TPU v7x, 512 devices: a whole 4x4x16 slice. The times are simulated.
512 devices in a mesh: occ: 64 (over x, z_lo, y), slab: 8 (over z_hi, core).
Axes of the slice: x: 4, y: 4, z: 16 (z_hi: 4, z_lo: 4; z = z_hi * 4 + z_lo), core: 2. Of those that a mesh axis runs over, the one named last changes fastest.
Arguments:
- amplitudes: bfloat16 [65536, 6144], P('occ', 'slab'), may hold values from -6 to 6
- integrals: bfloat16 [1024, 6144], P('occ', 'slab'), may hold values from -0.078125 to 0.078125
- prior_amplitudes: bfloat16 [1024, 65536], P('slab', 'occ'), may hold values from -1.796875 to 1.796875
- occ_counts: int32 [64], replicated, may hold values from 1 to 4, 160 in all
- occ_energy: float32 [160], replicated, may hold values from -2 to -0.5
- pair_orbitals: int32 [2, 512], replicated, may hold values from 0 to 999
- virt_energy: float32 [1000], replicated, may hold values from 0.1 to 4
Outputs:
- new_amps: float32 [1024, 65536], P('slab', 'occ')
Inputs may be any that keep to these rules, and one draw needn't show every extreme that they name: occ_counts sums to 160; some block holds exactly 4.
All inputs are finite; a program needn't handle non-finite values.
Results may differ from a plain program's by a relative error of at most 0.0003.
Values may be sent and summed in bfloat16 or wider, within the bound.
A program may use at most 64 MiB of HBM per device.

v0:
```python
import jax
import jax.numpy as jnp
from jax import lax
from jax.sharding import PartitionSpec as P

CAPI = 4
GROUP = 128


def mirror_columns(values):
    shape = values.shape
    grouped = values.reshape((shape[0] // GROUP, 2, GROUP // 2) + shape[1:])
    return grouped[:, ::-1].reshape(shape)


def per_device(
    amplitudes, integrals, prior_amplitudes, occ_counts, occ_energy, pair_orbitals, virt_energy
):
    slot_count = occ_counts.shape[0] * CAPI
    row_count = amplitudes.shape[0]
    slab_width = prior_amplitudes.shape[0]
    gathered = lax.all_gather(integrals, "occ", axis=0, tiled=True)
    total_width = gathered.shape[0]
    direct = lax.psum_scatter(
        lax.dot_general(
            gathered, amplitudes, (((1,), (1,)), ((), ())), preferred_element_type=jnp.float32
        ),
        "slab",
        scatter_dimension=0,
        tiled=True,
    )
    blocks = direct.reshape(slab_width, CAPI, slot_count)
    swapped = lax.all_to_all(blocks, "occ", split_axis=2, concat_axis=1, tiled=True)
    paired_contraction = blocks + jnp.transpose(mirror_columns(swapped), (0, 2, 1))
    offsets = jnp.cumsum(occ_counts) - occ_counts
    within = jnp.arange(CAPI, dtype=jnp.int32)
    orbital = (offsets[:, None] + within[None, :]).reshape(-1)
    live = (within[None, :] < occ_counts[:, None]).reshape(-1)
    match = orbital[:, None] == jnp.arange(occ_energy.shape[0], dtype=jnp.int32)[None, :]
    slot_energy = jnp.where(live, jnp.sum(jnp.where(match, occ_energy[None, :], 0.0), axis=1), 0.0)
    first_slot = lax.axis_index("occ") * CAPI
    mine_energy = lax.dynamic_slice_in_dim(slot_energy, first_slot, CAPI, 0)
    mine_live = lax.dynamic_slice_in_dim(live, first_slot, CAPI, 0)
    labels = jnp.arange(virt_energy.shape[0], dtype=jnp.int32)[None, :]
    first_energy = jnp.sum(
        jnp.where(pair_orbitals[0][:, None] == labels, virt_energy[None, :], 0.0), axis=1
    )
    second_energy = jnp.sum(
        jnp.where(pair_orbitals[1][:, None] == labels, virt_energy[None, :], 0.0), axis=1
    )
    half_sum = (first_energy + second_energy).reshape(total_width // GROUP, 1, GROUP // 2)
    pair_energy = jnp.broadcast_to(half_sum, (total_width // GROUP, 2, GROUP // 2)).reshape(
        total_width
    )
    local_pairs = lax.dynamic_slice_in_dim(
        pair_energy, lax.axis_index("slab") * slab_width, slab_width, 0
    )
    energy_denominator = (
        mine_energy[None, :, None] + slot_energy[None, None, :] - local_pairs[:, None, None]
    )
    both_live = (mine_live[:, None] & live[None, :])[None]
    refreshed_amplitudes = (
        prior_amplitudes.reshape(slab_width, CAPI, slot_count).astype(jnp.float32)
        + paired_contraction / energy_denominator
    )
    return jnp.where(both_live, refreshed_amplitudes, 0.0).reshape(slab_width, row_count)


def solution(mesh):
    return jax.shard_map(
        per_device,
        mesh=mesh,
        in_specs=(P("occ", "slab"), P("occ", "slab"), P("slab", "occ"), P(), P(), P(), P()),
        out_specs=P("slab", "occ"),
        check_vma=False,
    )
```

profile of v0, /device:TPU:1, one launch (start us, length us, event | category | flops | bytes accessed | tf_op | source)
XLA Modules:
  0.0 524.3 jit_solution(12420992048704135039)
XLA Ops:
  6.5 0.7 all-gather.2.cloned.1.call-update
  7.3 316.2 %all-gather.2.cloned.1.call-done = bf16[1024,768]{1,0:T(8,128)(2,1)} async-done(((bf16[16,768]{1,0:T(8,128)(2,1)}), bf16[1024,768]{1,0:T(8,128)(2,1)}) %all-gather.2.cloned.1.call-update) | async-done | bytes 1572880 | tf_op jit(solution)/shard_map/all_gather | solution.py:22
  323.5 5.2 fusion.3
  328.8 150.5 %reduce-scatter.2.cloned.1.call-done = f32[128,1024]{1,0:T(8,128)} async-done(((f32[1024,1024]{1,0:T(8,128)}), f32[128,1024]{1,0:T(8,128)}) %reduce-scatter.2.cloned.1.call-update) | async-done | bytes 524304 | tf_op jit(solution)/shard_map/reduce_scatter | solution.py:24
  479.2 1.3 reshape.163
  480.5 1.0 copy.37
  481.5 11.1 %all-to-all-start = ((f32[128,4,256]{0,1,2:T(4,128)}), f32[128,4,256]{0,1,2:T(4,128)S(1)}, u32[]{:S(2)}, u32[]{:S(2)}) async-start(f32[128,4,256]{0,1,2:T(4,128)} %copy.37), calls=%async_computation.1 | async-start | bytes 1048576 | tf_op jit(solution)/shard_map/all_to_all | solution.py:33
  492.7 0.1 iota_compare_fusion.3
  492.7 0.1 lt.37
  492.9 0.1 copy.43
  493.0 0.1 reduce-window.9
  493.1 0.1 reduce
  493.2 0.1 iota_add_fusion
  493.3 0.1 add.65
  493.4 0.1 dynamic_slice.9
  493.5 0.1 select_reduce_fusion.2
  493.6 0.1 dynamic_slice.10
  493.7 0.5 select_reduce_fusion
  494.2 0.1 add.70
  494.3 0.1 reshape.168
  494.4 0.2 copy.36
  494.5 0.1 dynamic_slice.11
  494.6 0.1 broadcast_and_fusion
  494.8 1.0 copy.42
  495.8 13.7 %all-to-all-done = f32[128,4,256]{0,1,2:T(4,128)S(1)} async-done(((f32[128,4,256]{0,1,2:T(4,128)}), f32[128,4,256]{0,1,2:T(4,128)S(1)}, u32[]{:S(2)}, u32[]{:S(2)}) %all-to-all-start) | async-done | bytes 524320 | tf_op jit(solution)/shard_map/all_to_all | solution.py:33
  509.5 0.1 copy.39
  509.6 0.7 reshape.164
  510.3 4.2 rev.3
  514.5 1.4 copy.40
  515.9 0.2 copy.41
  516.1 0.3 fusion
  516.5 1.0 copy.44
  (24 shorter events, 0.2 us)
Async XLA Ops:
  6.5 317.0 %copy-start = (bf16[1024,768]{1,0:T(8,128)(2,1)S(1)}, bf16[1024,768]{1,0:T(8,128)(2,1)}, u32[]{:S(2)}) copy-start(bf16[1024,768]{1,0:T(8,128)(2,1)} %param.7) | copy-start | bytes 4718596
  6.5 317.0 %all-gather.2.cloned.1.call-start = ((), (), s32[]{:S(2)}) async-start(), calls=%async_computation.2 | async-start | bytes 1597440 | tf_op jit(solution)/shard_map/all_gather | solution.py:22
  7.3 472.0 %reduce-scatter.2.cloned.1.call-start = ((), (), s32[]{:S(2)}) async-start(), calls=%async_computation.3 | async-start | bytes 4718592 | tf_op jit(solution)/shard_map/reduce_scatter | solution.py:24
  328.7 164.0 %copy-start.5 = (s32[64]{0:T(128)S(1)}, s32[64]{0:T(128)}, u32[]{:S(2)}) copy-start(s32[64]{0:T(128)} %param.10) | copy-start | bytes 772
  328.7 164.8 %copy-start.6 = (f32[160]{0:T(256)S(1)}, f32[160]{0:T(256)}, u32[]{:S(2)}) copy-start(f32[160]{0:T(256)} %param.11) | copy-start | bytes 1924
  328.7 164.9 %copy-start.4 = (s32[2,512]{1,0:T(2,128)S(1)}, s32[2,512]{1,0:T(2,128)}, u32[]{:S(2)}) copy-start(s32[2,512]{1,0:T(2,128)} %param.12) | copy-start | bytes 12292
  328.7 164.9 %copy-start.3 = (f32[1000]{0:T(1024)S(1)}, f32[1000]{0:T(1024)}, u32[]{:S(2)}) copy-start(f32[1000]{0:T(1024)} %param.13) | copy-start | bytes 12004
  328.7 165.6 %copy-start.2 = (bf16[128,1024]{1,0:T(8,128)(2,1)S(1)}, bf16[128,1024]{1,0:T(8,128)(2,1)}, u32[]{:S(2)}) copy-start(bf16[128,1024]{1,0:T(8,128)(2,1)} %param.9) | copy-start | bytes 786436
  481.5 27.9 %all-to-all-start = ((f32[128,4,256]{0,1,2:T(4,128)}), f32[128,4,256]{0,1,2:T(4,128)S(1)}, u32[]{:S(2)}, u32[]{:S(2)}) async-start(f32[128,4,256]{0,1,2:T(4,128)} %copy.37), calls=%async_computation.1 | async-start | bytes 1048576 | tf_op jit(solution)/shard_map/all_to_all | solution.py:33
  510.3 5.8 %copy-start.1 = (f32[128,4,256]{0,2,1:T(8,128)S(1)}, f32[128,4,256]{0,2,1:T(8,128)}, u32[]{:S(2)}) copy-start(f32[128,4,256]{0,2,1:T(8,128)} %copy.42) | copy-start | bytes 1572868
Sparse Core Ops, SparseCore 0:
  9.4 314.0 all-gather.1
  328.8 150.3 reduce-scatter.1
where the time goes:
time: 525 us; the launch traced here: 524 us
  waiting for transfers between devices  481 us (92%)
  between operations  13.6 us (3%)
  local copies, waits for them, and re-layouts  11.9 us (2%)
  starting transfers between devices  11.2 us (2%)
    all_gather x1, waiting for transfers between devices, per_device(): gathered = lax.all_gather(integrals, 'occ', axis=0, tiled=True)  316 us
    reduce_scatter x1, waiting for transfers between devices, per_device(): lax.psum_scatter(lax.dot_general(gathered, amplitudes, (((1,), (1,)), (()...  150 us
    all_to_all x1, waiting for transfers between devices, per_device(): lax.all_to_all(blocks, 'occ', split_axis=2, concat_axis=1, tiled=True)  13.7 us
    all_to_all x1, starting transfers between devices, per_device(): lax.all_to_all(blocks, 'occ', split_axis=2, concat_axis=1, tiled=True)  11.1 us
  transfers between devices with their start and end apart: 3, of which 3 were waited for; matrix products, arithmetic and copies ran while one was open for 1% of the time, Pallas kernels for 0%

commit v1 on v0

v1 whole, which is shorter than its diff:
```python
import functools

import jax
import jax.numpy as jnp
from jax import lax
from jax.experimental import pallas as pl
from jax.experimental.pallas import tpu as pltpu
from jax.sharding import PartitionSpec as P

CAPI = 4
GROUP = 128
NOCC = 160
SLOTS = 256
LIVE = CAPI * NOCC
MESH = pl.DeviceIdType.MESH
F32 = jnp.float32
BF16 = jnp.bfloat16


def halves(values):
    high = values.astype(BF16)
    return high, (values - high.astype(F32)).astype(BF16)


def dot_nt(left, right):
    return lax.dot_general(left, right, (((1,), (1,)), ((), ())), preferred_element_type=F32)


def dot_nn(left, right):
    return jnp.dot(left, right, preferred_element_type=F32)


def kernel(
    orb_ref, energy_ref, pair_ref, v_hbm, a_hbm, prior_hbm, out_ref,
    vb, amps, prior, packed, onehot, part, core_in, summed, ladder,
    up_out, down_out, up_in, down_in, up2_out, down2_out, up2_in, down2_in,
    turned, arrived,
    local_sem, z_send, z_recv, x_send, x_recv, y_send, y_recv, f_send, f_recv,
    c_send, c_recv, r_send, r_recv, e_send, e_recv,
):
    o = lax.axis_index("occ")
    s = lax.axis_index("slab")
    x, zl, y = o // 16, (o // 4) % 4, o % 4
    h, core = s // 2, s % 2
    other = 1 - core

    def at(value):
        return lax.rem(value + 8, 4)

    def place(px, pzl, py):
        return px * 16 + pzl * 4 + py

    def remote(src, dst, send, recv, occ, slab):
        return pltpu.make_async_remote_copy(
            src_ref=src, dst_ref=dst, send_sem=send, recv_sem=recv,
            device_id=(occ, slab), device_id_type=MESH,
        )

    sends = []

    def start(src, dst, send, recv, occ, slab):
        copy = remote(src, dst, send, recv, occ, slab)
        copy.start()
        sends.append(copy)

    def landed(dst, send, recv):
        remote(dst, dst, send, recv, lax.rem(o + 1, 64), s).wait_recv()

    get_v = pltpu.make_async_copy(v_hbm, vb.at[y, x, zl], local_sem.at[0])
    get_a = pltpu.make_async_copy(a_hbm, amps, local_sem.at[1])
    get_prior = pltpu.make_async_copy(prior_hbm, prior, local_sem.at[2])
    get_v.start()
    get_a.start()
    get_prior.start()

    barrier = pltpu.get_barrier_semaphore()

    def greet(t, carry):
        pl.semaphore_signal(
            barrier, inc=1, device_id=(lax.rem(o + t, 64), s), device_id_type=MESH
        )
        return carry

    lax.fori_loop(1, 64, greet, 0)
    up, down = 2 * at(h + 1) + core, 2 * at(h - 1) + core
    sibling = 2 * h + other
    for slab in (up, down, sibling):
        pl.semaphore_signal(barrier, inc=1, device_id=(o, slab), device_id_type=MESH)
    get_v.wait()
    pl.semaphore_wait(barrier, 66)

    for d in (1, 2, 3):
        start(vb.at[y, x, zl], vb.at[y, x, zl], z_send.at[d], z_recv.at[d], place(x, at(zl + d), y), s)

    match = lax.broadcasted_iota(jnp.int32, (NOCC, SLOTS), 0) == orb_ref[...]
    pick = jnp.where(match, 1.0, 0.0).astype(BF16)
    get_a.wait()
    for i in range(CAPI):
        packed[i * NOCC:(i + 1) * NOCC, :] = dot_nn(
            pick, amps[i * SLOTS:(i + 1) * SLOTS, :]
        ).astype(BF16)

    for d in (1, 2, 3):
        landed(vb.at[y, x, at(zl - d)], z_send.at[d], z_recv.at[d])

    x_next, x_back = place(at(x + 1), zl, y), place(at(x - 1), zl, y)
    y_next, y_back = place(x, zl, at(y + 1)), place(x, zl, at(y - 1))
    offsets = (0, -1, 1, 2)

    def y_piece(n):
        ref = vb.at[y, at(x + offsets[n])]
        start(ref, ref, y_send.at[n], y_recv.at[n], y_next, s)
        start(ref, ref, y_send.at[4 + n], y_recv.at[4 + n], y_back, s)

    def y_forward(n):
        px = at(x + offsets[n])
        landed(vb.at[at(y - 1), px], y_send.at[n], y_recv.at[n])
        ref = vb.at[at(y - 1), px, pl.ds(0, 2)]
        start(ref, ref, f_send.at[n], f_recv.at[n], y_next, s)
        landed(vb.at[at(y + 1), px], y_send.at[4 + n], y_recv.at[4 + n])
        ref = vb.at[at(y + 1), px, pl.ds(2, 2)]
        start(ref, ref, f_send.at[4 + n], f_recv.at[4 + n], y_back, s)

    ref = vb.at[y, x]
    start(ref, ref, x_send.at[0], x_recv.at[0], x_next, s)
    start(ref, ref, x_send.at[1], x_recv.at[1], x_back, s)
    y_piece(0)
    landed(vb.at[y, at(x - 1)], x_send.at[0], x_recv.at[0])
    ref = vb.at[y, at(x - 1), pl.ds(0, 2)]
    start(ref, ref, x_send.at[2], x_recv.at[2], x_next, s)
    landed(vb.at[y, at(x + 1)], x_send.at[1], x_recv.at[1])
    ref = vb.at[y, at(x + 1), pl.ds(2, 2)]
    start(ref, ref, x_send.at[3], x_recv.at[3], x_back, s)
    y_piece(1)
    y_piece(2)
    landed(vb.at[y, at(x + 2), pl.ds(0, 2)], x_send.at[2], x_recv.at[2])
    landed(vb.at[y, at(x + 2), pl.ds(2, 2)], x_send.at[3], x_recv.at[3])
    y_piece(3)

    steps = (0, 1, -1, 2)

    def multiply(t):
        block = vb[at(y + steps[t])].reshape(256, vb.shape[-1])
        part[t] = dot_nt(block, packed[...]).reshape(4, 2, 32, LIVE)
        start(part.at[t, :, other], core_in.at[t], c_send.at[t], c_recv.at[t], o, sibling)

    def add_cores(t):
        landed(core_in.at[t], c_send.at[t], c_recv.at[t])
        summed[t] = part[t, :, core] + core_in[t]
        up_out[t, 0] = summed[t, at(h + 1), 0:16]
        up_out[t, 1] = summed[t, at(h + 2), 16:32]
        down_out[t, 0] = summed[t, at(h - 2), 0:16]
        down_out[t, 1] = summed[t, at(h - 1), 16:32]
        start(up_out.at[t], up_in.at[t], r_send.at[t], r_recv.at[t], o, up)
        start(down_out.at[t], down_in.at[t], r_send.at[4 + t], r_recv.at[4 + t], o, down)

    def second(t):
        landed(up_in.at[t], r_send.at[t], r_recv.at[t])
        up2_out[t] = summed[t, at(h + 1), 16:32] + up_in[t, 1]
        start(up2_out.at[t], up2_in.at[t], r_send.at[8 + t], r_recv.at[8 + t], o, up)
        landed(down_in.at[t], r_send.at[4 + t], r_recv.at[4 + t])
        down2_out[t] = summed[t, at(h - 1), 0:16] + down_in[t, 0]
        start(down2_out.at[t], down2_in.at[t], r_send.at[12 + t], r_recv.at[12 + t], o, down)

    def finish(t):
        landed(up2_in.at[t], r_send.at[8 + t], r_recv.at[8 + t])
        landed(down2_in.at[t], r_send.at[12 + t], r_recv.at[12 + t])
        row = at(y + steps[t])
        ladder[0, row] = summed[t, h, 0:16] + up_in[t, 0] + down2_in[t]
        ladder[1, row] = summed[t, h, 16:32] + down_in[t, 1] + up2_in[t]

    multiply(0)
    y_forward(0)
    add_cores(0)
    y_forward(1)
    y_forward(2)
    y_forward(3)
    multiply(1)
    multiply(2)
    second(0)
    add_cores(1)
    add_cores(2)

    row_id = lax.broadcasted_iota(jnp.int32, (1024, SLOTS), 0)
    lane_id = lax.broadcasted_iota(jnp.int32, (1024, SLOTS), 1)
    orbital = jnp.sum(
        jnp.where(lane_id == (row_id >> 2), orb_ref[...].astype(F32), 0.0), axis=1, keepdims=True
    ).astype(jnp.int32)
    slot_i = lax.broadcasted_iota(jnp.int32, (1024, 1), 0) & 3
    column = jnp.where(orbital >= 0, slot_i * NOCC + orbital, -1)
    onehot[...] = jnp.where(
        lax.broadcasted_iota(jnp.int32, (1024, LIVE), 1) == column, 1.0, 0.0
    ).astype(BF16)

    for n in range(4):
        px = at(x + offsets[n])
        landed(vb.at[at(y + 2), px, pl.ds(0, 2)], f_send.at[n], f_recv.at[n])
        landed(vb.at[at(y + 2), px, pl.ds(2, 2)], f_send.at[4 + n], f_recv.at[4 + n])
    multiply(3)
    second(1)
    second(2)
    add_cores(3)
    finish(0)
    finish(1)
    finish(2)
    second(3)
    finish(3)

    low = ladder[0].reshape(GROUP // 2, LIVE)
    top = ladder[1].reshape(GROUP // 2, LIVE)
    high, rest = halves(jnp.concatenate([top, low], axis=0))
    turned[...] = dot_nt(onehot[...], high) + dot_nt(onehot[...], rest)

    def rows(b):
        return pl.ds(pl.multiple_of(b * 16, 16), 16)

    def exchange(t, b):
        return remote(
            turned.at[rows(b)], arrived.at[rows(o)], e_send.at[t], e_recv.at[t], b, s
        )

    def send(t, carry):
        exchange(t, lax.rem(o + t, 64)).start()
        return carry

    lax.fori_loop(1, 64, send, 0)
    arrived[rows(o), :] = turned[rows(o), :]

    high, rest = halves(jnp.concatenate([low, top], axis=0))
    own = []
    for q in range(CAPI):
        cut = slice(q * NOCC, (q + 1) * NOCC)
        own.append(dot_nn(high[:, cut], pick) + dot_nn(rest[:, cut], pick))
    get_prior.wait()

    spread = jnp.where(
        lax.broadcasted_iota(jnp.int32, (SLOTS, SLOTS), 1)
        == ((lax.broadcasted_iota(jnp.int32, (SLOTS, SLOTS), 0) & 63) * 4
            + (lax.broadcasted_iota(jnp.int32, (SLOTS, SLOTS), 0) >> 6)),
        1.0, 0.0,
    ).astype(BF16)

    for copy in sends:
        copy.wait_send()

    def receive(t, carry):
        b = lax.rem(o + 64 - t, 64)
        remote(arrived.at[rows(b)], arrived.at[rows(b)], e_send.at[t], e_recv.at[t], b, s).wait_recv()
        exchange(t, lax.rem(o + t, 64)).wait_send()
        return carry

    lax.fori_loop(1, 64, receive, 0)

    slot_id = lax.broadcasted_iota(jnp.int32, (1, SLOTS), 1)
    live = jnp.where(orb_ref[...] >= 0, 1.0, 0.0)
    for q in range(CAPI):
        block = jnp.concatenate(
            [arrived[pl.ds(q * CAPI + i, 64, stride=16), :] for i in range(CAPI)], axis=0
        )
        high, rest = halves(jnp.transpose(block))
        paired = own[q] + (dot_nn(high, spread) + dot_nn(rest, spread))
        mine = slot_id == o * CAPI + q
        energy = jnp.sum(jnp.where(mine, energy_ref[...], 0.0), axis=1, keepdims=True)
        alive = jnp.sum(jnp.where(mine, live, 0.0), axis=1, keepdims=True)
        cut = slice(q * SLOTS, (q + 1) * SLOTS)
        fresh = prior[:, cut].astype(F32) + paired / ((energy + energy_ref[...]) - pair_ref[...])
        out_ref[:, cut] = jnp.where(alive * live > 0.5, fresh, 0.0)


def per_device(
    amplitudes, integrals, prior_amplitudes, occ_counts, occ_energy, pair_orbitals, virt_energy
):
    depth = amplitudes.shape[1]
    offsets = jnp.cumsum(occ_counts) - occ_counts
    within = jnp.arange(CAPI, dtype=jnp.int32)
    live = (within[None, :] < occ_counts[:, None]).reshape(-1)
    orbital = jnp.where(live, (offsets[:, None] + within[None, :]).reshape(-1), -1)
    match = orbital[:, None] == jnp.arange(NOCC, dtype=jnp.int32)[None, :]
    slot_energy = jnp.sum(jnp.where(match, occ_energy[None, :], 0.0), axis=1)
    labels = jnp.arange(virt_energy.shape[0], dtype=jnp.int32)[None, :]
    mine = lax.dynamic_slice_in_dim(
        pair_orbitals, lax.axis_index("slab") * (GROUP // 2), GROUP // 2, 1
    )
    virtual = jnp.sum(
        jnp.where(mine[:, :, None] == labels[None], virt_energy[None, None, :], 0.0), axis=2
    )
    half_sum = virtual[0] + virtual[1]
    pair_energy = jnp.concatenate([half_sum, half_sum])[:, None]
    any_spec = pl.BlockSpec(memory_space=pl.ANY)
    vmem_spec = pl.BlockSpec(memory_space=pltpu.VMEM)
    dma = pltpu.SemaphoreType.DMA
    return pl.pallas_call(
        kernel,
        out_shape=jax.ShapeDtypeStruct((GROUP, CAPI * SLOTS), F32),
        in_specs=[vmem_spec] * 3 + [any_spec] * 3,
        out_specs=vmem_spec,
        scratch_shapes=[
            pltpu.VMEM((4, 4, 4, 16, depth), BF16),
            pltpu.VMEM((CAPI * SLOTS, depth), BF16),
            pltpu.VMEM((GROUP, CAPI * SLOTS), BF16),
            pltpu.VMEM((LIVE, depth), BF16),
            pltpu.VMEM((1024, LIVE), BF16),
            pltpu.VMEM((4, 4, 2, 32, LIVE), F32),
            pltpu.VMEM((4, 4, 32, LIVE), F32),
            pltpu.VMEM((4, 4, 32, LIVE), F32),
            pltpu.VMEM((2, 4, 16, LIVE), F32),
        ]
        + [pltpu.VMEM((4, 2, 16, LIVE), F32)] * 4
        + [pltpu.VMEM((4, 16, LIVE), F32)] * 4
        + [pltpu.VMEM((1024, GROUP), F32)] * 2
        + [
            dma((3,)), dma((4,)), dma((4,)), dma((4,)), dma((4,)), dma((8,)), dma((8,)), dma((8,)), dma((8,)),
            dma((4,)), dma((4,)), dma((16,)), dma((16,)), dma((64,)), dma((64,)),
        ],
        compiler_params=pltpu.CompilerParams(
            collective_id=0, has_side_effects=True, vmem_limit_bytes=44 * 1024 * 1024
        ),
        cost_estimate=pl.CostEstimate(flops=2 * 1024 * 640 * 768, bytes_accessed=3 << 20, transcendentals=0),
    )(orbital[None, :], slot_energy[None, :], pair_energy, integrals, amplitudes, prior_amplitudes)


def solution(mesh):
    return jax.shard_map(
        per_device,
        mesh=mesh,
        in_specs=(P("occ", "slab"), P("occ", "slab"), P("slab", "occ"), P(), P(), P(), P()),
        out_specs=P("slab", "occ"),
        check_vma=False,
    )
```

time: 525 us -> 106 us (0.20)
  waiting for transfers between devices: 481 us -> 0 us
  Pallas kernels: 0 us -> 96.8 us
  between operations: 13.6 us -> 0.04 us
  starting transfers between devices: 11.2 us -> 0 us
  local copies, waits for them, and re-layouts: 11.9 us -> 5.72 us
    all_gather x1 -> x0, waiting for transfers between devices: 316 us -> none  [per_device(): gathered = lax.all_gather(integrals, 'occ', axis=0, tiled=True)]
    reduce_scatter x1 -> x0, waiting for transfers between devices: 150 us -> none  [per_device(): lax.psum_scatter(lax.dot_general(gathered, amplitudes, (((1,), (1,)), (()...]
    pallas_call x0 -> x1, Pallas kernels: none -> 96.8 us  [per_device(): pl.pallas_call(kernel, out_shape=jax.ShapeDtypeStruct((GROUP, CAPI * SLOT...]
    all_to_all x1 -> x0, waiting for transfers between devices: 13.7 us -> none  [per_device(): lax.all_to_all(blocks, 'occ', split_axis=2, concat_axis=1, tiled=True)]
    all_to_all x1 -> x0, starting transfers between devices: 11.1 us -> none  [per_device(): lax.all_to_all(blocks, 'occ', split_axis=2, concat_axis=1, tiled=True)]
    rev x2 -> x0, local copies, waits for them, and re-layouts: 5.62 us -> none  [mirror_columns(): return grouped[:, ::-1].reshape(shape)]
    reshape x7 -> x0, local copies, waits for them, and re-layouts: 5.29 us -> none  [the longest x3 3.34 us: per_device(): blocks = direct.reshape(slab_width, CAPI, slot_count)]
  transfers between devices with their start and end apart: 3 -> 0, of which waited for: 3 -> 0; matrix products, arithmetic and copies ran while one was open for 1% -> 0% of each run, Pallas kernels for 0% -> 0%
where the time goes in v1:
time: 106 us
  Pallas kernels  96.8 us (91%)
  local copies, waits for them, and re-layouts  5.72 us (5%)
  other arithmetic  3.36 us (3%)
    pallas_call x1, Pallas kernels, per_device(): pl.pallas_call(kernel, out_shape=jax.ShapeDtypeStruct((GROUP, CAPI * SLOT...  96.8 us
    unnamed x9, local copies, waits for them, and re-layouts  4.57 us

profile of v1, /device:TPU:1, one launch (start us, length us, event | category | flops | bytes accessed | tf_op | source)
XLA Modules:
  0.0 105.9 jit_solution(2371392083107346848)
XLA Ops:
  0.0 0.0 copy-start
  0.0 0.7 copy-done
  0.7 0.1 constant_dynamic-slice_fusion
  0.8 0.9 select_reduce_fusion
  1.7 0.1 maximum_bitcast_fusion
  1.7 0.8 copy.12
  2.5 0.1 reduce-window.9
  2.6 0.1 reduce
  2.7 0.7 sub.3
  3.4 0.7 add_select_fusion
  4.1 0.1 select_n.34
  4.2 0.1 select_n.33.orb_ref
  4.3 0.8 select_reduce_fusion.1
  5.1 0.1 copy.13.pair_ref
  5.2 0.0 copy-start.1
  5.2 1.4 %copy-done.1 = bf16[1024,768]{1,0:T(8,128)(2,1)S(1)} copy-done((bf16[1024,768]{1,0:T(8,128)(2,1)S(1)}, bf16[1024,768]{1,0:T(8,128)(2,1)}, u32[]{:S(2)}) %copy-start.1) | copy-done | bytes 1572888
  6.6 0.0 copy-start.2
  6.6 0.9 copy-done.2
  7.6 0.0 copy-start.3
  7.6 0.7 copy-done.3
  8.3 96.8 %shard_map.73 = f32[128,1024]{1,0:T(8,128)S(1)} custom-call(s32[1,256]{1,0:T(1,128)S(1)} %select_n.33.orb_ref, f32[1,256]{1,0:T(1,128)S(1)} %bitcast.6, f32[128,1]{1,0:T(8,128)S(1)} %copy.13.pair_ref, bf16[16,768]{1,0:T(8,128)(2,1)S(1)} %copy-done.3, bf16[1024,768]{1,0:T(8,128)(2,1)S(1)} %copy-done.1, bf16[128,1024]{1,0:T(8,128)(2,1)S(1)} %copy-done.2), custom_call_target="tpu_custom_call" | custom-call | flops 1006632960 | bytes 3145728 | tf_op jit(solution)/shard_map/pallas_call | solution.py:292
  105.1 0.8 copy.15
  (1 shorter events, 0.0 us)
Async XLA Ops:
  0.0 0.7 copy-start
  5.2 1.4 %copy-start.1 = (bf16[1024,768]{1,0:T(8,128)(2,1)S(1)}, bf16[1024,768]{1,0:T(8,128)(2,1)}, u32[]{:S(2)}) copy-start(bf16[1024,768]{1,0:T(8,128)(2,1)} %a_hbm.1) | copy-start | bytes 4718596
  6.6 0.9 copy-start.2
  7.6 0.7 copy-start.3

commit v2 on v1

--- a/solution.py
+++ b/solution.py
@@ -31,12 +31,13 @@
 
 
 def kernel(
-    orb_ref, energy_ref, pair_ref, v_hbm, a_hbm, prior_hbm, out_ref,
-    vb, amps, prior, packed, onehot, part, core_in, summed, ladder,
+    v_hbm, a_hbm, prior_hbm, counts_hbm, occ_hbm, pairs_hbm, virt_hbm, out_ref,
+    vb, amps, prior, counts, occ_energy, pairs, virt, packed, onehot, part, core_in, summed, ladder,
     up_out, down_out, up_in, down_in, up2_out, down2_out, up2_in, down2_in,
+    up_top, down_top, up_top_in, down_top_in, up2_top, down2_top, up2_top_in, down2_top_in,
     turned, arrived,
     local_sem, z_send, z_recv, x_send, x_recv, y_send, y_recv, f_send, f_recv,
-    c_send, c_recv, r_send, r_recv, e_send, e_recv,
+    c_send, c_recv, r_send, r_recv, m_send, m_recv, e_send, e_recv,
 ):
     o = lax.axis_index("occ")
     s = lax.axis_index("slab")
@@ -69,30 +70,46 @@
     get_v = pltpu.make_async_copy(v_hbm, vb.at[y, x, zl], local_sem.at[0])
     get_a = pltpu.make_async_copy(a_hbm, amps, local_sem.at[1])
     get_prior = pltpu.make_async_copy(prior_hbm, prior, local_sem.at[2])
+    small = [
+        pltpu.make_async_copy(src, dst, local_sem.at[3 + n])
+        for n, (src, dst) in enumerate(
+            ((counts_hbm, counts), (occ_hbm, occ_energy), (pairs_hbm, pairs), (virt_hbm, virt))
+        )
+    ]
     get_v.start()
+    for copy in small:
+        copy.start()
     get_a.start()
     get_prior.start()
 
     barrier = pltpu.get_barrier_semaphore()
 
-    def greet(t, carry):
-        pl.semaphore_signal(
-            barrier, inc=1, device_id=(lax.rem(o + t, 64), s), device_id_type=MESH
-        )
-        return carry
-
-    lax.fori_loop(1, 64, greet, 0)
     up, down = 2 * at(h + 1) + core, 2 * at(h - 1) + core
     sibling = 2 * h + other
-    for slab in (up, down, sibling):
-        pl.semaphore_signal(barrier, inc=1, device_id=(o, slab), device_id_type=MESH)
+    x_next, x_back = place(at(x + 1), zl, y), place(at(x - 1), zl, y)
+    y_next, y_back = place(x, zl, at(y + 1)), place(x, zl, at(y - 1))
+    partners = [(place(x, at(zl + d), y), s) for d in (1, 2, 3)]
+    partners += [(x_next, s), (x_back, s), (y_next, s), (y_back, s)]
+    partners += [(o, up), (o, down), (o, sibling)]
+    for partner in partners:
+        pl.semaphore_signal(barrier, inc=1, device_id=partner, device_id_type=MESH)
     get_v.wait()
-    pl.semaphore_wait(barrier, 66)
+    pl.semaphore_wait(barrier, len(partners))
 
     for d in (1, 2, 3):
         start(vb.at[y, x, zl], vb.at[y, x, zl], z_send.at[d], z_recv.at[d], place(x, at(zl + d), y), s)
 
-    match = lax.broadcasted_iota(jnp.int32, (NOCC, SLOTS), 0) == orb_ref[...]
+    for copy in small:
+        copy.wait()
+    slot_id = lax.broadcasted_iota(jnp.int32, (1, SLOTS), 1)
+    block_id = lax.broadcasted_iota(jnp.int32, (64, SLOTS), 0)
+    block_of = lax.broadcasted_iota(jnp.int32, (64, SLOTS), 1) >> 2
+    held = jnp.broadcast_to(counts[...].astype(F32), (8, 64)).astype(BF16)
+    before = dot_nn(held, jnp.where(block_id < block_of, 1.0, 0.0).astype(BF16))[0:1]
+    own_count = dot_nn(held, jnp.where(block_id == block_of, 1.0, 0.0).astype(BF16))[0:1]
+    within = (slot_id & 3).astype(F32)
+    orbital_row = jnp.where(within < own_count, before + within, -1.0)
+    match = lax.broadcasted_iota(jnp.int32, (NOCC, SLOTS), 0).astype(F32) == orbital_row
     pick = jnp.where(match, 1.0, 0.0).astype(BF16)
     get_a.wait()
     for i in range(CAPI):
@@ -100,11 +117,29 @@
             pick, amps[i * SLOTS:(i + 1) * SLOTS, :]
         ).astype(BF16)
 
+    rest = jnp.broadcast_to(occ_energy[...], (8, NOCC))
+    energy_row = jnp.zeros((8, SLOTS), F32)
+    for _ in range(3):
+        piece = rest.astype(BF16)
+        rest = rest - piece.astype(F32)
+        energy_row = energy_row + dot_nn(piece, pick)
+    energy_row = energy_row[0:1]
+    pair_total = pairs.shape[1]
+    wanted = s * (GROUP // 2) + (lax.broadcasted_iota(jnp.int32, (GROUP, pair_total), 0) & 63)
+    chosen = lax.broadcasted_iota(jnp.int32, (GROUP, pair_total), 1) == wanted
+    label = lax.broadcasted_iota(jnp.int32, (GROUP, virt.shape[1]), 1).astype(F32)
+    pair_energy = jnp.zeros((GROUP, 1), F32)
+    for n in range(2):
+        orbital = jnp.sum(
+            jnp.where(chosen, pairs[n:n + 1, :].astype(F32), 0.0), axis=1, keepdims=True
+        )
+        pair_energy = pair_energy + jnp.sum(
+            jnp.where(label == orbital, virt[...], 0.0), axis=1, keepdims=True
+        )
+
     for d in (1, 2, 3):
         landed(vb.at[y, x, at(zl - d)], z_send.at[d], z_recv.at[d])
 
-    x_next, x_back = place(at(x + 1), zl, y), place(at(x - 1), zl, y)
-    y_next, y_back = place(x, zl, at(y + 1)), place(x, zl, at(y - 1))
     offsets = (0, -1, 1, 2)
 
     def y_piece(n):
@@ -144,30 +179,60 @@
         part[t] = dot_nt(block, packed[...]).reshape(4, 2, 32, LIVE)
         start(part.at[t, :, other], core_in.at[t], c_send.at[t], c_recv.at[t], o, sibling)
 
+    eye = lax.broadcasted_iota(jnp.int32, (32, GROUP), 0) == lax.broadcasted_iota(
+        jnp.int32, (32, GROUP), 1
+    )
+
+    def code(values, out, top_out):
+        rows = values.shape[0]
+        top = jnp.maximum(jnp.max(jnp.abs(values), axis=1, keepdims=True), 1e-30)
+        coded = jnp.round(values * (32767.0 / top)).astype(jnp.int32).astype(jnp.int16)
+        out[...] = coded.reshape(out.shape)
+        top_out[...] = jnp.sum(jnp.where(eye[:rows], top, 0.0), axis=0, keepdims=True)
+
+    def decode(coded, top_row):
+        rows = coded.shape[0]
+        top = jnp.sum(jnp.where(eye[:rows], top_row, 0.0), axis=1, keepdims=True)
+        return coded.astype(F32) * (top * (1.0 / 32767.0))
+
+    def send_coded(n, values, out, top_out, into, top_into, slab):
+        code(values, out, top_out)
+        start(out, into, r_send.at[n], r_recv.at[n], o, slab)
+        start(top_out, top_into, m_send.at[n], m_recv.at[n], o, slab)
+
+    def landed_coded(n, into, top_into):
+        landed(into, r_send.at[n], r_recv.at[n])
+        landed(top_into, m_send.at[n], m_recv.at[n])
+        return decode(into[...].reshape(-1, LIVE), top_into[...])
+
     def add_cores(t):
         landed(core_in.at[t], c_send.at[t], c_recv.at[t])
         summed[t] = part[t, :, core] + core_in[t]
-        up_out[t, 0] = summed[t, at(h + 1), 0:16]
-        up_out[t, 1] = summed[t, at(h + 2), 16:32]
-        down_out[t, 0] = summed[t, at(h - 2), 0:16]
-        down_out[t, 1] = summed[t, at(h - 1), 16:32]
-        start(up_out.at[t], up_in.at[t], r_send.at[t], r_recv.at[t], o, up)
-        start(down_out.at[t], down_in.at[t], r_send.at[4 + t], r_recv.at[4 + t], o, down)
+        up_values = jnp.concatenate([summed[t, at(h + 1), 0:16], summed[t, at(h + 2), 16:32]])
+        send_coded(t, up_values, up_out.at[t], up_top.at[t], up_in.at[t], up_top_in.at[t], up)
+        down_values = jnp.concatenate([summed[t, at(h - 2), 0:16], summed[t, at(h - 1), 16:32]])
+        send_coded(
+            4 + t, down_values, down_out.at[t], down_top.at[t], down_in.at[t], down_top_in.at[t], down
+        )
 
     def second(t):
-        landed(up_in.at[t], r_send.at[t], r_recv.at[t])
-        up2_out[t] = summed[t, at(h + 1), 16:32] + up_in[t, 1]
-        start(up2_out.at[t], up2_in.at[t], r_send.at[8 + t], r_recv.at[8 + t], o, up)
-        landed(down_in.at[t], r_send.at[4 + t], r_recv.at[4 + t])
-        down2_out[t] = summed[t, at(h - 1), 0:16] + down_in[t, 0]
-        start(down2_out.at[t], down2_in.at[t], r_send.at[12 + t], r_recv.at[12 + t], o, down)
+        values = landed_coded(t, up_in.at[t], up_top_in.at[t])
+        summed[t, h, 0:16] = summed[t, h, 0:16] + values[0:16]
+        send_coded(
+            8 + t, summed[t, at(h + 1), 16:32] + values[16:32],
+            up2_out.at[t], up2_top.at[t], up2_in.at[t], up2_top_in.at[t], up,
+        )
+        values = landed_coded(4 + t, down_in.at[t], down_top_in.at[t])
+        summed[t, h, 16:32] = summed[t, h, 16:32] + values[16:32]
+        send_coded(
+            12 + t, summed[t, at(h - 1), 0:16] + values[0:16],
+            down2_out.at[t], down2_top.at[t], down2_in.at[t], down2_top_in.at[t], down,
+        )
 
     def finish(t):
-        landed(up2_in.at[t], r_send.at[8 + t], r_recv.at[8 + t])
-        landed(down2_in.at[t], r_send.at[12 + t], r_recv.at[12 + t])
         row = at(y + steps[t])
-        ladder[0, row] = summed[t, h, 0:16] + up_in[t, 0] + down2_in[t]
-        ladder[1, row] = summed[t, h, 16:32] + down_in[t, 1] + up2_in[t]
+        ladder[0, row] = summed[t, h, 0:16] + landed_coded(12 + t, down2_in.at[t], down2_top_in.at[t])
+        ladder[1, row] = summed[t, h, 16:32] + landed_coded(8 + t, up2_in.at[t], up2_top_in.at[t])
 
     multiply(0)
     y_forward(0)
@@ -184,7 +249,7 @@
     row_id = lax.broadcasted_iota(jnp.int32, (1024, SLOTS), 0)
     lane_id = lax.broadcasted_iota(jnp.int32, (1024, SLOTS), 1)
     orbital = jnp.sum(
-        jnp.where(lane_id == (row_id >> 2), orb_ref[...].astype(F32), 0.0), axis=1, keepdims=True
+        jnp.where(lane_id == (row_id >> 2), orbital_row, 0.0), axis=1, keepdims=True
     ).astype(jnp.int32)
     slot_i = lax.broadcasted_iota(jnp.int32, (1024, 1), 0) & 3
     column = jnp.where(orbital >= 0, slot_i * NOCC + orbital, -1)
@@ -251,8 +316,7 @@
 
     lax.fori_loop(1, 64, receive, 0)
 
-    slot_id = lax.broadcasted_iota(jnp.int32, (1, SLOTS), 1)
-    live = jnp.where(orb_ref[...] >= 0, 1.0, 0.0)
+    live = jnp.where(orbital_row >= 0.0, 1.0, 0.0)
     for q in range(CAPI):
         block = jnp.concatenate(
             [arrived[pl.ds(q * CAPI + i, 64, stride=16), :] for i in range(CAPI)], axis=0
@@ -260,10 +324,10 @@
         high, rest = halves(jnp.transpose(block))
         paired = own[q] + (dot_nn(high, spread) + dot_nn(rest, spread))
         mine = slot_id == o * CAPI + q
-        energy = jnp.sum(jnp.where(mine, energy_ref[...], 0.0), axis=1, keepdims=True)
+        energy = jnp.sum(jnp.where(mine, energy_row, 0.0), axis=1, keepdims=True)
         alive = jnp.sum(jnp.where(mine, live, 0.0), axis=1, keepdims=True)
         cut = slice(q * SLOTS, (q + 1) * SLOTS)
-        fresh = prior[:, cut].astype(F32) + paired / ((energy + energy_ref[...]) - pair_ref[...])
+        fresh = prior[:, cut].astype(F32) + paired / ((energy + energy_row) - pair_energy)
         out_ref[:, cut] = jnp.where(alive * live > 0.5, fresh, 0.0)
 
 
@@ -271,33 +335,23 @@
     amplitudes, integrals, prior_amplitudes, occ_counts, occ_energy, pair_orbitals, virt_energy
 ):
     depth = amplitudes.shape[1]
-    offsets = jnp.cumsum(occ_counts) - occ_counts
-    within = jnp.arange(CAPI, dtype=jnp.int32)
-    live = (within[None, :] < occ_counts[:, None]).reshape(-1)
-    orbital = jnp.where(live, (offsets[:, None] + within[None, :]).reshape(-1), -1)
-    match = orbital[:, None] == jnp.arange(NOCC, dtype=jnp.int32)[None, :]
-    slot_energy = jnp.sum(jnp.where(match, occ_energy[None, :], 0.0), axis=1)
-    labels = jnp.arange(virt_energy.shape[0], dtype=jnp.int32)[None, :]
-    mine = lax.dynamic_slice_in_dim(
-        pair_orbitals, lax.axis_index("slab") * (GROUP // 2), GROUP // 2, 1
-    )
-    virtual = jnp.sum(
-        jnp.where(mine[:, :, None] == labels[None], virt_energy[None, None, :], 0.0), axis=2
-    )
-    half_sum = virtual[0] + virtual[1]
-    pair_energy = jnp.concatenate([half_sum, half_sum])[:, None]
+    pair_count, virt_count = pair_orbitals.shape[1], virt_energy.shape[0]
     any_spec = pl.BlockSpec(memory_space=pl.ANY)
     vmem_spec = pl.BlockSpec(memory_space=pltpu.VMEM)
     dma = pltpu.SemaphoreType.DMA
     return pl.pallas_call(
         kernel,
         out_shape=jax.ShapeDtypeStruct((GROUP, CAPI * SLOTS), F32),
-        in_specs=[vmem_spec] * 3 + [any_spec] * 3,
+        in_specs=[any_spec] * 7,
         out_specs=vmem_spec,
         scratch_shapes=[
             pltpu.VMEM((4, 4, 4, 16, depth), BF16),
             pltpu.VMEM((CAPI * SLOTS, depth), BF16),
             pltpu.VMEM((GROUP, CAPI * SLOTS), BF16),
+            pltpu.VMEM((1, occ_counts.shape[0]), jnp.int32),
+            pltpu.VMEM((1, NOCC), F32),
+            pltpu.VMEM((2, pair_count), jnp.int32),
+            pltpu.VMEM((1, virt_count), F32),
             pltpu.VMEM((LIVE, depth), BF16),
             pltpu.VMEM((1024, LIVE), BF16),
             pltpu.VMEM((4, 4, 2, 32, LIVE), F32),
@@ -305,18 +359,22 @@
             pltpu.VMEM((4, 4, 32, LIVE), F32),
             pltpu.VMEM((2, 4, 16, LIVE), F32),
         ]
-        + [pltpu.VMEM((4, 2, 16, LIVE), F32)] * 4
-        + [pltpu.VMEM((4, 16, LIVE), F32)] * 4
+        + [pltpu.VMEM((4, 2, 16, LIVE), jnp.int16)] * 4
+        + [pltpu.VMEM((4, 16, LIVE), jnp.int16)] * 4
+        + [pltpu.VMEM((4, 1, GROUP), F32)] * 8
         + [pltpu.VMEM((1024, GROUP), F32)] * 2
         + [
-            dma((3,)), dma((4,)), dma((4,)), dma((4,)), dma((4,)), dma((8,)), dma((8,)), dma((8,)), dma((8,)),
-            dma((4,)), dma((4,)), dma((16,)), dma((16,)), dma((64,)), dma((64,)),
+            dma((7,)), dma((4,)), dma((4,)), dma((4,)), dma((4,)), dma((8,)), dma((8,)), dma((8,)), dma((8,)),
+            dma((4,)), dma((4,)), dma((16,)), dma((16,)), dma((16,)), dma((16,)), dma((64,)), dma((64,)),
         ],
         compiler_params=pltpu.CompilerParams(
-            collective_id=0, has_side_effects=True, vmem_limit_bytes=44 * 1024 * 1024
+            collective_id=0, has_side_effects=True, vmem_limit_bytes=60 * 1024 * 1024
         ),
         cost_estimate=pl.CostEstimate(flops=2 * 1024 * 640 * 768, bytes_accessed=3 << 20, transcendentals=0),
-    )(orbital[None, :], slot_energy[None, :], pair_energy, integrals, amplitudes, prior_amplitudes)
+    )(
+        integrals, amplitudes, prior_amplitudes,
+        occ_counts[None, :], occ_energy[None, :], pair_orbitals, virt_energy[None, :],
+    )
 
 
 def solution(mesh):

time: 106 us -> 78.9 us (0.74)
  the two profiles are of different devices: /device:TPU:1 before, /device:TPU:2 now
where the time goes in v2:
time: 78.9 us; the launch traced here: 78.7 us
  Pallas kernels  76.8 us (97%)
  local copies, waits for them, and re-layouts  1.89 us (2%)
    pallas_call x1, Pallas kernels, per_device(): pl.pallas_call(kernel, out_shape=jax.ShapeDtypeStruct((GROUP, CAPI * SLOT...  76.8 us
    unnamed x1, local copies, waits for them, and re-layouts  1.89 us

profile of v2, /device:TPU:2, one launch (start us, length us, event | category | flops | bytes accessed | tf_op | source)
XLA Modules:
  0.0 78.7 jit_solution(15706507832701861959)
XLA Ops:
  0.0 76.8 %shard_map.73 = f32[128,1024]{1,0:T(8,128)} custom-call(bf16[16,768]{1,0:T(8,128)(2,1)} %v_hbm.1, bf16[1024,768]{1,0:T(8,128)(2,1)} %a_hbm.1, bf16[128,1024]{1,0:T(8,128)(2,1)} %prior_hbm.1, s32[1,64]{1,0:T(1,128)} %bitcast.5, f32[1,160]{1,0:T(1,128)} %bitcast.4, s32[2,512]{1,0:T(2,128)} %pairs_hbm.1, f32[1,1000]{1,0:T(1,128)} %bitcast.3), custom_call_target="tpu_custom_call" | custom-call | flops 1006632960 | bytes 3145728 | tf_op jit(solution)/shard_map/pallas_call | solution.py:342
  76.8 1.9 %copy.9 = f32[128,1024]{1,0:T(8,128)} copy(f32[128,1024]{1,0:T(8,128)} %shard_map.73) | data formatting | bytes 1048576

commit v3 on v2

v3 whole, which is shorter than its diff:
```python
import functools

import jax
import jax.numpy as jnp
from jax import lax
from jax.experimental import pallas as pl
from jax.experimental.pallas import tpu as pltpu
from jax.sharding import PartitionSpec as P

CAPI = 4
GROUP = 128
NOCC = 160
SLOTS = 256
LIVE = CAPI * NOCC
MESH = pl.DeviceIdType.MESH
F32 = jnp.float32
BF16 = jnp.bfloat16


def halves(values):
    high = values.astype(BF16)
    return high, (values - high.astype(F32)).astype(BF16)


def dot_nt(left, right):
    return lax.dot_general(left, right, (((1,), (1,)), ((), ())), preferred_element_type=F32)


def dot_nn(left, right):
    return jnp.dot(left, right, preferred_element_type=F32)


def kernel(
    v_hbm, a_hbm, prior_hbm, counts_hbm, occ_hbm, pairs_hbm, virt_hbm, out_ref,
    vb, amps, prior, counts, occ_energy, pairs, virt, packed, onehot, part, core_in, summed, ladder,
    r_out, r_in, top_out, top_in,
    turned, arrived, peaks, opened,
    local_sem, z_send, z_recv, y_send, y_recv, f_send, f_recv,
    c_send, c_recv, r_send, r_recv, m_send, m_recv, e_send, e_recv, p_send, p_recv,
):
    o = lax.axis_index("occ")
    s = lax.axis_index("slab")
    x, zl, y = o // 16, (o // 4) % 4, o % 4
    h, core = s // 2, s % 2
    other = 1 - core

    def at(value):
        return lax.rem(value + 8, 4)

    def place(px, pzl, py):
        return px * 16 + pzl * 4 + py

    def remote(src, dst, send, recv, occ, slab):
        return pltpu.make_async_remote_copy(
            src_ref=src, dst_ref=dst, send_sem=send, recv_sem=recv,
            device_id=(occ, slab), device_id_type=MESH,
        )

    sends = []

    def start(src, dst, send, recv, occ, slab):
        copy = remote(src, dst, send, recv, occ, slab)
        copy.start()
        sends.append(copy)

    def landed(dst, send, recv):
        remote(dst, dst, send, recv, lax.rem(o + 1, 64), s).wait_recv()

    barrier = pltpu.get_barrier_semaphore()
    up, down = 2 * at(h + 1) + core, 2 * at(h - 1) + core
    sibling = 2 * h + other
    y_next, y_back = place(x, zl, at(y + 1)), place(x, zl, at(y - 1))
    partners = [(place(x, at(zl + d), y), s) for d in (1, 2, 3)]
    partners += [(place(at(x + d), zl, y), s) for d in (1, 2, 3)]
    partners += [(y_next, s), (y_back, s)]
    partners += [(o, up), (o, down), (o, sibling)]
    for partner in partners:
        pl.semaphore_signal(barrier, inc=1, device_id=partner, device_id_type=MESH)

    get_v = pltpu.make_async_copy(v_hbm, vb.at[y, zl % 2, x, zl // 2], local_sem.at[0])
    get_a = pltpu.make_async_copy(a_hbm, amps, local_sem.at[1])
    get_prior = pltpu.make_async_copy(prior_hbm, prior, local_sem.at[2])
    small = [
        pltpu.make_async_copy(src, dst, local_sem.at[3 + n])
        for n, (src, dst) in enumerate(
            ((counts_hbm, counts), (occ_hbm, occ_energy), (pairs_hbm, pairs), (virt_hbm, virt))
        )
    ]
    get_v.start()
    for copy in small:
        copy.start()
    get_a.start()
    get_prior.start()

    get_v.wait()
    pl.semaphore_wait(barrier, len(partners))

    def block_at(px, pzl):
        return vb.at[y, pzl % 2, px, pzl // 2]

    for d in (2, 1, 3):
        start(
            block_at(x, zl), block_at(x, zl), z_send.at[d], z_recv.at[d], place(x, at(zl + d), y), s
        )
    for d in (2, 1, 3):
        landed(block_at(x, at(zl - d)), z_send.at[d], z_recv.at[d])
    for k in (0, 1):
        for dx in (2, 1, 3):
            n = 4 + 4 * k + dx
            start(
                vb.at[y, k, x], vb.at[y, k, x], z_send.at[n], z_recv.at[n], place(at(x + dx), zl, y), s
            )

    for copy in small:
        copy.wait()
    slot_id = lax.broadcasted_iota(jnp.int32, (1, SLOTS), 1)
    block_id = lax.broadcasted_iota(jnp.int32, (64, SLOTS), 0)
    block_of = lax.broadcasted_iota(jnp.int32, (64, SLOTS), 1) >> 2
    held = jnp.broadcast_to(counts[...].astype(F32), (8, 64)).astype(BF16)
    before = dot_nn(held, jnp.where(block_id < block_of, 1.0, 0.0).astype(BF16))[0:1]
    own_count = dot_nn(held, jnp.where(block_id == block_of, 1.0, 0.0).astype(BF16))[0:1]
    within = (slot_id & 3).astype(F32)
    orbital_row = jnp.where(within < own_count, before + within, -1.0)
    match = lax.broadcasted_iota(jnp.int32, (NOCC, SLOTS), 0).astype(F32) == orbital_row
    pick = jnp.where(match, 1.0, 0.0).astype(BF16)
    get_a.wait()
    for i in range(CAPI):
        packed[i * NOCC:(i + 1) * NOCC, :] = dot_nn(
            pick, amps[i * SLOTS:(i + 1) * SLOTS, :]
        ).astype(BF16)

    def own_row(k):
        for dx in (2, 1, 3):
            n = 4 + 4 * k + dx
            landed(vb.at[y, k, at(x - dx)], z_send.at[n], z_recv.at[n])
        ref = vb.at[y, k]
        start(ref, ref, y_send.at[k], y_recv.at[k], y_next, s)
        start(ref, ref, y_send.at[2 + k], y_recv.at[2 + k], y_back, s)

    def forward(k):
        landed(vb.at[at(y - 1), k], y_send.at[k], y_recv.at[k])
        ref = vb.at[at(y - 1), k, pl.ds(0, 2)]
        start(ref, ref, f_send.at[k], f_recv.at[k], y_next, s)
        landed(vb.at[at(y + 1), k], y_send.at[2 + k], y_recv.at[2 + k])
        ref = vb.at[at(y + 1), k, pl.ds(2, 2)]
        start(ref, ref, f_send.at[2 + k], f_recv.at[2 + k], y_back, s)

    def far_row(k):
        landed(vb.at[at(y + 2), k, pl.ds(0, 2)], f_send.at[k], f_recv.at[k])
        landed(vb.at[at(y + 2), k, pl.ds(2, 2)], f_send.at[2 + k], f_recv.at[2 + k])

    parts = ((0, 0), (0, 1), (1, 0), (-1, 0), (1, 1), (-1, 1), (2, 0), (2, 1))

    def multiply(*ts):
        blocks = []
        for t in ts:
            step, k = parts[t]
            blocks.append(vb[at(y + step), k].reshape(128, vb.shape[-1]))
        product = dot_nt(jnp.concatenate(blocks, axis=0), packed[...])
        for n, t in enumerate(ts):
            part[t] = product[128 * n:128 * (n + 1)].reshape(4, 2, 16, LIVE)
            start(part.at[t, :, other], core_in.at[t], c_send.at[t], c_recv.at[t], o, sibling)

    eye = lax.broadcasted_iota(jnp.int32, (16, GROUP), 0) == lax.broadcasted_iota(
        jnp.int32, (16, GROUP), 1
    )

    def code(values, out, top_out):
        top = jnp.maximum(jnp.max(jnp.abs(values), axis=1, keepdims=True), 1e-30)
        out[...] = jnp.round(values * (32767.0 / top)).astype(jnp.int32).astype(jnp.int16)
        top_out[...] = jnp.sum(jnp.where(eye, top, 0.0), axis=0, keepdims=True)

    def decode(coded, top_row):
        top = jnp.sum(jnp.where(eye, top_row, 0.0), axis=1, keepdims=True)
        return coded.astype(F32) * (top * (1.0 / 32767.0))

    def ahead(t):
        return (up, 1) if t % 2 else (down, -1)

    def behind(t):
        return ahead(t + 1)

    def send_coded(n, values, slab):
        code(values, r_out.at[n], top_out.at[n])
        start(r_out.at[n], r_in.at[n], r_send.at[n], r_recv.at[n], o, slab)
        start(top_out.at[n], top_in.at[n], m_send.at[n], m_recv.at[n], o, slab)

    def landed_coded(n):
        landed(r_in.at[n], r_send.at[n], r_recv.at[n])
        landed(top_in.at[n], m_send.at[n], m_recv.at[n])
        return decode(r_in[n], top_in[n])

    def add_cores(t):
        landed(core_in.at[t], c_send.at[t], c_recv.at[t])
        summed[t] = part[t, :, core] + core_in[t]
        send_coded(3 * t, summed[t, at(h + 2)], ahead(t)[0])
        slab, step = behind(t)
        send_coded(3 * t + 1, summed[t, at(h + step)], slab)

    def second(t):
        slab, step = ahead(t)
        values = summed[t, at(h + step)] + landed_coded(3 * t)
        send_coded(3 * t + 2, values, slab)

    def finish(t):
        step, k = parts[t]
        ladder[k, at(y + step)] = (
            summed[t, h] + landed_coded(3 * t + 1) + landed_coded(3 * t + 2)
        )

    own_row(0)
    multiply(0)
    own_row(1)
    multiply(1)
    add_cores(0)
    add_cores(1)

    rest = jnp.broadcast_to(occ_energy[...], (8, NOCC))
    energy_row = jnp.zeros((8, SLOTS), F32)
    for _ in range(3):
        piece = rest.astype(BF16)
        rest = rest - piece.astype(F32)
        energy_row = energy_row + dot_nn(piece, pick)
    energy_row = energy_row[0:1]
    pair_total = pairs.shape[1]
    wanted = s * (GROUP // 2) + (lax.broadcasted_iota(jnp.int32, (GROUP, pair_total), 0) & 63)
    chosen = lax.broadcasted_iota(jnp.int32, (GROUP, pair_total), 1) == wanted
    label = lax.broadcasted_iota(jnp.int32, (GROUP, virt.shape[1]), 1).astype(F32)
    pair_energy = jnp.zeros((GROUP, 1), F32)
    for n in range(2):
        orbital = jnp.sum(
            jnp.where(chosen, pairs[n:n + 1, :].astype(F32), 0.0), axis=1, keepdims=True
        )
        pair_energy = pair_energy + jnp.sum(
            jnp.where(label == orbital, virt[...], 0.0), axis=1, keepdims=True
        )

    row_id = lax.broadcasted_iota(jnp.int32, (1024, SLOTS), 0)
    lane_id = lax.broadcasted_iota(jnp.int32, (1024, SLOTS), 1)
    orbital = jnp.sum(
        jnp.where(lane_id == (row_id >> 2), orbital_row, 0.0), axis=1, keepdims=True
    ).astype(jnp.int32)
    slot_i = lax.broadcasted_iota(jnp.int32, (1024, 1), 0) & 3
    column = jnp.where(orbital >= 0, slot_i * NOCC + orbital, -1)
    onehot[...] = jnp.where(
        lax.broadcasted_iota(jnp.int32, (1024, LIVE), 1) == column, 1.0, 0.0
    ).astype(BF16)

    forward(0)
    multiply(2, 3)
    add_cores(2)
    add_cores(3)
    forward(1)
    multiply(4, 5)
    add_cores(4)
    add_cores(5)
    far_row(0)
    multiply(6)
    add_cores(6)
    far_row(1)
    multiply(7)
    add_cores(7)
    for t in range(8):
        second(t)
    for t in range(8):
        finish(t)

    low = ladder[0].reshape(GROUP // 2, LIVE)
    top = ladder[1].reshape(GROUP // 2, LIVE)
    mirrored = jnp.concatenate([top, low], axis=0)
    peak = jnp.maximum(jnp.max(jnp.abs(mirrored), axis=1, keepdims=True), 1e-30)
    diagonal = lax.broadcasted_iota(jnp.int32, (GROUP, GROUP), 0) == lax.broadcasted_iota(
        jnp.int32, (GROUP, GROUP), 1
    )
    peaks[o] = jnp.sum(jnp.where(diagonal, peak, 0.0), axis=0, keepdims=True)

    def rows(b):
        return pl.ds(pl.multiple_of(b * 16, 16), 16)

    def exchange_peak(t, b):
        return remote(peaks.at[o], peaks.at[o], p_send.at[t], p_recv.at[t], b, s)

    def exchange(t, b):
        return remote(
            turned.at[rows(b)], arrived.at[rows(o)], e_send.at[t], e_recv.at[t], b, s
        )

    def send_peak(t, carry):
        exchange_peak(t, lax.rem(o + t, 64)).start()
        return carry

    def send(t, carry):
        exchange(t, lax.rem(o + t, 64)).start()
        return carry

    lax.fori_loop(1, 64, send_peak, 0)
    whole = jnp.round(mirrored * (32767.0 / peak))
    coarse = jnp.round(whole * (1.0 / 256.0))
    fine = (whole - 256.0 * coarse).astype(BF16)
    turned[...] = (
        256.0 * dot_nt(onehot[...], coarse.astype(BF16)) + dot_nt(onehot[...], fine)
    ).astype(jnp.int32).astype(jnp.int16)
    lax.fori_loop(1, 64, send, 0)
    arrived[rows(o), :] = turned[rows(o), :]

    high, rest = halves(jnp.concatenate([low, top], axis=0))
    own = []
    for q in range(CAPI):
        cut = slice(q * NOCC, (q + 1) * NOCC)
        own.append(dot_nn(high[:, cut], pick) + dot_nn(rest[:, cut], pick))
    get_prior.wait()

    spread = jnp.where(
        lax.broadcasted_iota(jnp.int32, (SLOTS, SLOTS), 1)
        == ((lax.broadcasted_iota(jnp.int32, (SLOTS, SLOTS), 0) & 63) * 4
            + (lax.broadcasted_iota(jnp.int32, (SLOTS, SLOTS), 0) >> 6)),
        1.0, 0.0,
    ).astype(BF16)

    for copy in sends:
        copy.wait_send()

    def receive(t, carry):
        b = lax.rem(o + 64 - t, 64)
        remote(arrived.at[rows(b)], arrived.at[rows(b)], e_send.at[t], e_recv.at[t], b, s).wait_recv()
        remote(peaks.at[b], peaks.at[b], p_send.at[t], p_recv.at[t], b, s).wait_recv()
        exchange(t, lax.rem(o + t, 64)).wait_send()
        exchange_peak(t, lax.rem(o + t, 64)).wait_send()
        return carry

    lax.fori_loop(1, 64, receive, 0)

    opened[...] = (
        arrived[...].astype(F32).reshape(64, 16, GROUP) * (peaks[...] * (1.0 / 32767.0))
    ).reshape(1024, GROUP)
    live = jnp.where(orbital_row >= 0.0, 1.0, 0.0)
    for q in range(CAPI):
        block = jnp.concatenate(
            [opened[pl.ds(q * CAPI + i, 64, stride=16), :] for i in range(CAPI)], axis=0
        )
        high, rest = halves(jnp.transpose(block))
        paired = own[q] + (dot_nn(high, spread) + dot_nn(rest, spread))
        mine = slot_id == o * CAPI + q
        energy = jnp.sum(jnp.where(mine, energy_row, 0.0), axis=1, keepdims=True)
        alive = jnp.sum(jnp.where(mine, live, 0.0), axis=1, keepdims=True)
        cut = slice(q * SLOTS, (q + 1) * SLOTS)
        fresh = prior[:, cut].astype(F32) + paired / ((energy + energy_row) - pair_energy)
        out_ref[:, cut] = jnp.where(alive * live > 0.5, fresh, 0.0)


def per_device(
    amplitudes, integrals, prior_amplitudes, occ_counts, occ_energy, pair_orbitals, virt_energy
):
    depth = amplitudes.shape[1]
    pair_count, virt_count = pair_orbitals.shape[1], virt_energy.shape[0]
    hbm_spec = pl.BlockSpec(memory_space=pltpu.HBM)
    vmem_spec = pl.BlockSpec(memory_space=pltpu.VMEM)
    dma = pltpu.SemaphoreType.DMA
    return pl.pallas_call(
        kernel,
        out_shape=pltpu.VMEM((GROUP, CAPI * SLOTS), F32),
        in_specs=[hbm_spec] * 7,
        out_specs=vmem_spec,
        scratch_shapes=[
            pltpu.VMEM((4, 2, 4, 2, 16, depth), BF16),
            pltpu.VMEM((CAPI * SLOTS, depth), BF16),
            pltpu.VMEM((GROUP, CAPI * SLOTS), BF16),
            pltpu.VMEM((1, occ_counts.shape[0]), jnp.int32),
            pltpu.VMEM((1, NOCC), F32),
            pltpu.VMEM((2, pair_count), jnp.int32),
            pltpu.VMEM((1, virt_count), F32),
            pltpu.VMEM((LIVE, depth), BF16),
            pltpu.VMEM((1024, LIVE), BF16),
            pltpu.VMEM((8, 4, 2, 16, LIVE), F32),
            pltpu.VMEM((8, 4, 16, LIVE), F32),
            pltpu.VMEM((8, 4, 16, LIVE), F32),
            pltpu.VMEM((2, 4, 16, LIVE), F32),
        ]
        + [pltpu.VMEM((24, 16, LIVE), jnp.int16)] * 2
        + [pltpu.VMEM((24, 1, GROUP), F32)] * 2
        + [pltpu.VMEM((1024, GROUP), jnp.int16)] * 2
        + [pltpu.VMEM((64, 1, GROUP), F32), pltpu.VMEM((1024, GROUP), F32)]
        + [
            dma((7,)), dma((16,)), dma((16,)), dma((8,)), dma((8,)), dma((8,)), dma((8,)),
            dma((8,)), dma((8,)), dma((24,)), dma((24,)), dma((24,)), dma((24,)), dma((64,)), dma((64,)),
            dma((64,)), dma((64,)),
        ],
        compiler_params=pltpu.CompilerParams(
            collective_id=0, has_side_effects=True, vmem_limit_bytes=58 * 1024 * 1024
        ),
        cost_estimate=pl.CostEstimate(flops=2 * 1024 * 640 * 768, bytes_accessed=3 << 20, transcendentals=0),
    )(
        integrals, amplitudes, prior_amplitudes,
        occ_counts[None, :], occ_energy[None, :], pair_orbitals, virt_energy[None, :],
    )


def solution(mesh):
    return jax.shard_map(
        per_device,
        mesh=mesh,
        in_specs=(P("occ", "slab"), P("occ", "slab"), P("slab", "occ"), P(), P(), P(), P()),
        out_specs=P("slab", "occ"),
        check_vma=False,
    )
```

time: 78.9 us -> 70.4 us (0.89)
  the two profiles are of different devices: /device:TPU:2 before, /device:TPU:1 now
where the time goes in v3:
time: 70.4 us; the launch traced here: 70.3 us
  Pallas kernels  69.5 us (99%)
  local copies, waits for them, and re-layouts  0.8 us (1%)
    pallas_call x1, Pallas kernels, per_device(): pl.pallas_call(kernel, out_shape=pltpu.VMEM((GROUP, CAPI * SLOTS), F32),...  69.5 us

profile of v3, /device:TPU:1, one launch (start us, length us, event | category | flops | bytes accessed | tf_op | source)
XLA Modules:
  0.0 70.3 jit_solution(17796020025441045527)
XLA Ops:
  0.0 69.5 %shard_map.73 = f32[128,1024]{1,0:T(8,128)S(1)} custom-call(bf16[16,768]{1,0:T(8,128)(2,1)} %v_hbm.1, bf16[1024,768]{1,0:T(8,128)(2,1)} %a_hbm.1, bf16[128,1024]{1,0:T(8,128)(2,1)} %prior_hbm.1, s32[1,64]{1,0:T(1,128)} %bitcast.5, f32[1,160]{1,0:T(1,128)} %bitcast.4, s32[2,512]{1,0:T(2,128)} %pairs_hbm.1, f32[1,1000]{1,0:T(1,128)} %bitcast.3), custom_call_target="tpu_custom_call" | custom-call | flops 1006632960 | bytes 3145728 | tf_op jit(solution)/shard_map/pallas_call | solution.py:359
  69.5 0.8 %copy.9 = f32[128,1024]{1,0:T(8,128)} copy(f32[128,1024]{1,0:T(8,128)S(1)} %shard_map.73) | data formatting | bytes 1048576

commit v4 on v3

--- a/solution.py
+++ b/solution.py
@@ -35,7 +35,8 @@
     vb, amps, prior, counts, occ_energy, pairs, virt, packed, onehot, part, core_in, summed, ladder,
     r_out, r_in, top_out, top_in,
     turned, arrived, peaks, opened,
-    local_sem, z_send, z_recv, y_send, y_recv, f_send, f_recv,
+    near_sem, far_sem,
+    local_sem, z_send, z_recv, x_send, x_recv, y_send, y_recv, f_send, f_recv, s_send, s_recv,
     c_send, c_recv, r_send, r_recv, m_send, m_recv, e_send, e_recv, p_send, p_recv,
 ):
     o = lax.axis_index("occ")
@@ -69,13 +70,41 @@
     barrier = pltpu.get_barrier_semaphore()
     up, down = 2 * at(h + 1) + core, 2 * at(h - 1) + core
     sibling = 2 * h + other
-    y_next, y_back = place(x, zl, at(y + 1)), place(x, zl, at(y - 1))
-    partners = [(place(x, at(zl + d), y), s) for d in (1, 2, 3)]
-    partners += [(place(at(x + d), zl, y), s) for d in (1, 2, 3)]
-    partners += [(y_next, s), (y_back, s)]
-    partners += [(o, up), (o, down), (o, sibling)]
-    for partner in partners:
-        pl.semaphore_signal(barrier, inc=1, device_id=partner, device_id_type=MESH)
+    near = [place(x, at(zl + d), y) for d in (1, 2, 3)]
+    near += [place(at(x + d), zl, y) for d in (1, 2, 3)]
+    near += [place(x, zl, at(y + d)) for d in (1, 2, 3)]
+
+    def greet(occ, slab):
+        pl.semaphore_signal(barrier, inc=1, device_id=(occ, slab), device_id_type=MESH)
+
+    greet(o, sibling)
+    for occ in near:
+        greet(occ, 2 * h)
+    for step in (1, -1):
+        greet(o, 2 * at(h + step) + 1)
+
+    def tell(sem):
+        pl.semaphore_signal(sem, inc=1, device_id=(o, sibling), device_id_type=MESH)
+
+    def meet_near():
+        @pl.when(core == 0)
+        def _():
+            pl.semaphore_wait(barrier, 2 * len(near) + 1)
+            tell(near_sem)
+
+        @pl.when(core == 1)
+        def _():
+            pl.semaphore_wait(near_sem, 1)
+
+    def meet_far():
+        @pl.when(core == 1)
+        def _():
+            pl.semaphore_wait(barrier, 5)
+            tell(far_sem)
+
+        @pl.when(core == 0)
+        def _():
+            pl.semaphore_wait(far_sem, 1)
 
     get_v = pltpu.make_async_copy(v_hbm, vb.at[y, zl % 2, x, zl // 2], local_sem.at[0])
     get_a = pltpu.make_async_copy(a_hbm, amps, local_sem.at[1])
@@ -93,7 +122,7 @@
     get_prior.start()
 
     get_v.wait()
-    pl.semaphore_wait(barrier, len(partners))
+    meet_near()
 
     def block_at(px, pzl):
         return vb.at[y, pzl % 2, px, pzl // 2]
@@ -104,12 +133,15 @@
         )
     for d in (2, 1, 3):
         landed(block_at(x, at(zl - d)), z_send.at[d], z_recv.at[d])
+
     for k in (0, 1):
-        for dx in (2, 1, 3):
-            n = 4 + 4 * k + dx
-            start(
-                vb.at[y, k, x], vb.at[y, k, x], z_send.at[n], z_recv.at[n], place(at(x + dx), zl, y), s
-            )
+        ref = vb.at[y, k, x]
+        for d in (2, 1, 3):
+            n = 4 * k + d
+            start(ref, ref, x_send.at[n], x_recv.at[n], place(at(x + d), zl, y), s)
+        for d in (1, 3, 2):
+            n = 4 * k + d
+            start(ref, ref, y_send.at[n], y_recv.at[n], place(x, zl, at(y + d)), s)
 
     for copy in small:
         copy.wait()
@@ -130,24 +162,28 @@
         ).astype(BF16)
 
     def own_row(k):
-        for dx in (2, 1, 3):
-            n = 4 + 4 * k + dx
-            landed(vb.at[y, k, at(x - dx)], z_send.at[n], z_recv.at[n])
-        ref = vb.at[y, k]
-        start(ref, ref, y_send.at[k], y_recv.at[k], y_next, s)
-        start(ref, ref, y_send.at[2 + k], y_recv.at[2 + k], y_back, s)
-
-    def forward(k):
-        landed(vb.at[at(y - 1), k], y_send.at[k], y_recv.at[k])
-        ref = vb.at[at(y - 1), k, pl.ds(0, 2)]
-        start(ref, ref, f_send.at[k], f_recv.at[k], y_next, s)
-        landed(vb.at[at(y + 1), k], y_send.at[2 + k], y_recv.at[2 + k])
-        ref = vb.at[at(y + 1), k, pl.ds(2, 2)]
-        start(ref, ref, f_send.at[2 + k], f_recv.at[2 + k], y_back, s)
-
-    def far_row(k):
-        landed(vb.at[at(y + 2), k, pl.ds(0, 2)], f_send.at[k], f_recv.at[k])
-        landed(vb.at[at(y + 2), k, pl.ds(2, 2)], f_send.at[2 + k], f_recv.at[2 + k])
+        for d in (2, 1, 3):
+            landed(vb.at[y, k, at(x - d)], x_send.at[4 * k + d], x_recv.at[4 * k + d])
+
+    def opposite(k):
+        ref = vb.at[y, k, at(x + 2)]
+        for d in (1, 3, 2):
+            n = 4 * k + d
+            start(ref, ref, f_send.at[n], f_recv.at[n], place(x, zl, at(y + d)), s)
+
+    def pass_on(k, d):
+        n = 4 * k + d
+        ref = vb.at[at(y - d), k, x]
+        landed(ref, y_send.at[n], y_recv.at[n])
+        start(ref, ref, s_send.at[2 * n], s_recv.at[2 * n], place(at(x + 1), zl, y), s)
+        start(ref, ref, s_send.at[2 * n + 1], s_recv.at[2 * n + 1], place(at(x - 1), zl, y), s)
+
+    def other_row(k, d):
+        n = 4 * k + d
+        row = at(y - d)
+        landed(vb.at[row, k, at(x + 2)], f_send.at[n], f_recv.at[n])
+        landed(vb.at[row, k, at(x - 1)], s_send.at[2 * n], s_recv.at[2 * n])
+        landed(vb.at[row, k, at(x + 1)], s_send.at[2 * n + 1], s_recv.at[2 * n + 1])
 
     parts = ((0, 0), (0, 1), (1, 0), (-1, 0), (1, 1), (-1, 1), (2, 0), (2, 1))
 
@@ -208,11 +244,20 @@
             summed[t, h] + landed_coded(3 * t + 1) + landed_coded(3 * t + 2)
         )
 
+    pass_on(0, 1)
+    pass_on(0, 3)
     own_row(0)
     multiply(0)
+    opposite(0)
+    pass_on(1, 1)
+    pass_on(1, 3)
     own_row(1)
     multiply(1)
+    opposite(1)
+    pass_on(0, 2)
+    meet_far()
     add_cores(0)
+    pass_on(1, 2)
     add_cores(1)
 
     rest = jnp.broadcast_to(occ_energy[...], (8, NOCC))
@@ -237,8 +282,9 @@
 
     row_id = lax.broadcasted_iota(jnp.int32, (1024, SLOTS), 0)
     lane_id = lax.broadcasted_iota(jnp.int32, (1024, SLOTS), 1)
+    wanted = (((row_id >> 6) & 3) << 6) + ((row_id >> 8) << 4) + ((row_id >> 2) & 15)
     orbital = jnp.sum(
-        jnp.where(lane_id == (row_id >> 2), orbital_row, 0.0), axis=1, keepdims=True
+        jnp.where(lane_id == wanted, orbital_row, 0.0), axis=1, keepdims=True
     ).astype(jnp.int32)
     slot_i = lax.broadcasted_iota(jnp.int32, (1024, 1), 0) & 3
     column = jnp.where(orbital >= 0, slot_i * NOCC + orbital, -1)
@@ -246,19 +292,11 @@
         lax.broadcasted_iota(jnp.int32, (1024, LIVE), 1) == column, 1.0, 0.0
     ).astype(BF16)
 
-    forward(0)
-    multiply(2, 3)
-    add_cores(2)
-    add_cores(3)
-    forward(1)
-    multiply(4, 5)
-    add_cores(4)
-    add_cores(5)
-    far_row(0)
-    multiply(6)
-    add_cores(6)
-    far_row(1)
-    multiply(7)
+    for t, k, d in ((2, 0, 3), (3, 0, 1), (4, 1, 3), (5, 1, 1), (6, 0, 2), (7, 1, 2)):
+        other_row(k, d)
+        multiply(t)
+        if t >= 3:
+            add_cores(t - 1)
     add_cores(7)
     for t in range(8):
         second(t)
@@ -277,31 +315,36 @@
     def rows(b):
         return pl.ds(pl.multiple_of(b * 16, 16), 16)
 
-    def exchange_peak(t, b):
-        return remote(peaks.at[o], peaks.at[o], p_send.at[t], p_recv.at[t], b, s)
-
-    def exchange(t, b):
-        return remote(
-            turned.at[rows(b)], arrived.at[rows(o)], e_send.at[t], e_recv.at[t], b, s
-        )
-
-    def send_peak(t, carry):
-        exchange_peak(t, lax.rem(o + t, 64)).start()
-        return carry
-
-    def send(t, carry):
-        exchange(t, lax.rem(o + t, 64)).start()
-        return carry
-
-    lax.fori_loop(1, 64, send_peak, 0)
+    def exchange(dx, d, dy, sign=1):
+        n = dx * 16 + d * 4 + dy
+        px, pzl, py = at(x + sign * dx), at(zl + sign * d), at(y + sign * dy)
+        b = place(px, pzl, py)
+        source = o if sign > 0 else b
+        return (
+            remote(
+                turned.at[rows(pzl * 16 + px * 4 + py)], arrived.at[rows(source)],
+                e_send.at[n], e_recv.at[n], b, s,
+            ),
+            remote(peaks.at[source], peaks.at[source], p_send.at[n], p_recv.at[n], b, s),
+        )
+
     whole = jnp.round(mirrored * (32767.0 / peak))
     coarse = jnp.round(whole * (1.0 / 256.0))
     fine = (whole - 256.0 * coarse).astype(BF16)
-    turned[...] = (
-        256.0 * dot_nt(onehot[...], coarse.astype(BF16)) + dot_nt(onehot[...], fine)
-    ).astype(jnp.int32).astype(jnp.int16)
-    lax.fori_loop(1, 64, send, 0)
-    arrived[rows(o), :] = turned[rows(o), :]
+    coarse = coarse.astype(BF16)
+    order = []
+    for d in (2, 1, 3, 0):
+        group = pl.ds(pl.multiple_of(at(zl + d) * 256, 256), 256)
+        turned[group, :] = (
+            256.0 * dot_nt(onehot[group, :], coarse) + dot_nt(onehot[group, :], fine)
+        ).astype(jnp.int32).astype(jnp.int16)
+        for dx in (2, 1, 3, 0):
+            for dy in (2, 1, 3, 0):
+                if dx or d or dy:
+                    order.append((dx, d, dy))
+                    for copy in exchange(dx, d, dy):
+                        copy.start()
+    arrived[rows(o), :] = turned[rows(zl * 16 + x * 4 + y), :]
 
     high, rest = halves(jnp.concatenate([low, top], axis=0))
     own = []
@@ -320,15 +363,11 @@
     for copy in sends:
         copy.wait_send()
 
-    def receive(t, carry):
-        b = lax.rem(o + 64 - t, 64)
-        remote(arrived.at[rows(b)], arrived.at[rows(b)], e_send.at[t], e_recv.at[t], b, s).wait_recv()
-        remote(peaks.at[b], peaks.at[b], p_send.at[t], p_recv.at[t], b, s).wait_recv()
-        exchange(t, lax.rem(o + t, 64)).wait_send()
-        exchange_peak(t, lax.rem(o + t, 64)).wait_send()
-        return carry
-
-    lax.fori_loop(1, 64, receive, 0)
+    for step in order:
+        for copy in exchange(*step, sign=-1):
+            copy.wait_recv()
+        for copy in exchange(*step):
+            copy.wait_send()
 
     opened[...] = (
         arrived[...].astype(F32).reshape(64, 16, GROUP) * (peaks[...] * (1.0 / 32767.0))
@@ -380,8 +419,10 @@
         + [pltpu.VMEM((24, 1, GROUP), F32)] * 2
         + [pltpu.VMEM((1024, GROUP), jnp.int16)] * 2
         + [pltpu.VMEM((64, 1, GROUP), F32), pltpu.VMEM((1024, GROUP), F32)]
+        + [pltpu.SemaphoreType.REGULAR] * 2
         + [
-            dma((7,)), dma((16,)), dma((16,)), dma((8,)), dma((8,)), dma((8,)), dma((8,)),
+            dma((7,)), dma((4,)), dma((4,)), dma((8,)), dma((8,)), dma((8,)), dma((8,)), dma((8,)), dma((8,)),
+            dma((16,)), dma((16,)),
             dma((8,)), dma((8,)), dma((24,)), dma((24,)), dma((24,)), dma((24,)), dma((64,)), dma((64,)),
             dma((64,)), dma((64,)),
         ],

time: 70.4 us -> 65.5 us (0.930)
  Pallas kernels: 69.5 us -> 64.2 us
    pallas_call x1, Pallas kernels: 69.5 us -> 64.2 us  [per_device(): pl.pallas_call(kernel, out_shape=pltpu.VMEM((GROUP, CAPI * SLOTS), F32),...]
where the time goes in v4:
time: 65.5 us; the launch traced here: 65 us
  Pallas kernels  64.2 us (98%)
  local copies, waits for them, and re-layouts  0.8 us (1%)
    pallas_call x1, Pallas kernels, per_device(): pl.pallas_call(kernel, out_shape=pltpu.VMEM((GROUP, CAPI * SLOTS), F32),...  64.2 us

profile of v4, /device:TPU:1, one launch (start us, length us, event | category | flops | bytes accessed | tf_op | source)
XLA Modules:
  0.0 65.0 jit_solution(3602891862002536945)
XLA Ops:
  0.0 64.2 %shard_map.73 = f32[128,1024]{1,0:T(8,128)S(1)} custom-call(bf16[16,768]{1,0:T(8,128)(2,1)} %v_hbm.1, bf16[1024,768]{1,0:T(8,128)(2,1)} %a_hbm.1, bf16[128,1024]{1,0:T(8,128)(2,1)} %prior_hbm.1, s32[1,64]{1,0:T(1,128)} %bitcast.5, f32[1,160]{1,0:T(1,128)} %bitcast.4, s32[2,512]{1,0:T(2,128)} %pairs_hbm.1, f32[1,1000]{1,0:T(1,128)} %bitcast.3), custom_call_target="tpu_custom_call" | custom-call | flops 1006632960 | bytes 3145728 | tf_op jit(solution)/shard_map/pallas_call | solution.py:398
  64.3 0.8 %copy.9 = f32[128,1024]{1,0:T(8,128)} copy(f32[128,1024]{1,0:T(8,128)S(1)} %shard_map.73) | data formatting | bytes 1048576

commit v5 on v4

--- a/solution.py
+++ b/solution.py
@@ -369,7 +369,7 @@
         for copy in exchange(*step):
             copy.wait_send()
 
-    opened[...] = (
+    opened[0:1024, :] = (
         arrived[...].astype(F32).reshape(64, 16, GROUP) * (peaks[...] * (1.0 / 32767.0))
     ).reshape(1024, GROUP)
     live = jnp.where(orbital_row >= 0.0, 1.0, 0.0)
@@ -418,7 +418,7 @@
         + [pltpu.VMEM((24, 16, LIVE), jnp.int16)] * 2
         + [pltpu.VMEM((24, 1, GROUP), F32)] * 2
         + [pltpu.VMEM((1024, GROUP), jnp.int16)] * 2
-        + [pltpu.VMEM((64, 1, GROUP), F32), pltpu.VMEM((1024, GROUP), F32)]
+        + [pltpu.VMEM((64, 1, GROUP), F32), pltpu.VMEM((1040, GROUP), F32)]
         + [pltpu.SemaphoreType.REGULAR] * 2
         + [
             dma((7,)), dma((4,)), dma((4,)), dma((8,)), dma((8,)), dma((8,)), dma((8,)), dma((8,)), dma((8,)),

time: 65.5 us -> 65.6 us (level)
  no operation moved by 1% of the time
where the time goes in v5:
time: 65.6 us; the launch traced here: 65 us
  Pallas kernels  64.2 us (98%)
  local copies, waits for them, and re-layouts  0.8 us (1%)
    pallas_call x1, Pallas kernels, per_device(): pl.pallas_call(kernel, out_shape=pltpu.VMEM((GROUP, CAPI * SLOTS), F32),...  64.2 us

profile of v5, /device:TPU:1, one launch (start us, length us, event | category | flops | bytes accessed | tf_op | source)
XLA Modules:
  0.0 65.0 jit_solution(9026386958125301477)
XLA Ops:
  0.0 64.2 %shard_map.73 = f32[128,1024]{1,0:T(8,128)S(1)} custom-call(bf16[16,768]{1,0:T(8,128)(2,1)} %v_hbm.1, bf16[1024,768]{1,0:T(8,128)(2,1)} %a_hbm.1, bf16[128,1024]{1,0:T(8,128)(2,1)} %prior_hbm.1, s32[1,64]{1,0:T(1,128)} %bitcast.5, f32[1,160]{1,0:T(1,128)} %bitcast.4, s32[2,512]{1,0:T(2,128)} %pairs_hbm.1, f32[1,1000]{1,0:T(1,128)} %bitcast.3), custom_call_target="tpu_custom_call" | custom-call | flops 1006632960 | bytes 3145728 | tf_op jit(solution)/shard_map/pallas_call | solution.py:398
  64.2 0.8 %copy.9 = f32[128,1024]{1,0:T(8,128)} copy(f32[128,1024]{1,0:T(8,128)S(1)} %shard_map.73) | data formatting | bytes 1048576
